TPU v7x, 32 devices: a whole 2x2x4 slice. The times are simulated.
32 devices in a mesh: members: 2 (over y), areal: 8 (over z, x), layer: 2 (over core).
Axes of the slice: x: 2, y: 2, z: 4, core: 2. Of those that a mesh axis runs over, the one named last changes fastest.
Arguments:
- pressure: float32 [32, 64, 512], P(('members', 'layer'), 'areal'), parts along dimension 0, may hold values from -6 to 6
- saturation: float32 [32, 64, 512], P(('members', 'layer'), 'areal'), parts along dimension 0, may hold values from 0.05 to 0.95
- sat_cotangent: float32 [32, 64, 512], P(('members', 'layer'), 'areal'), parts along dimension 0, may hold values from -12 to 12
- dt_over_pv: float32 [32, 64, 512], P(('members', 'layer'), 'areal'), parts along dimension 0, may hold values from 0.3 to 3
- compress: float32 [32, 64, 512], P(('members', 'layer'), 'areal'), parts along dimension 0, may hold values from 0.05 to 0.5
- trans: float32 [3, 32, 64, 512], P(None, ('members', 'layer'), 'areal'), parts along dimension 1, may hold values from 0.2 to 5
- cell_flags: int32 [32, 64, 512], P(('members', 'layer'), 'areal'), parts along dimension 0, may hold values from 0 to 15, as said below
- well_cells: int32 [128], P('members'), parts along dimension 0, may hold values from 0 to 524287
- well_misfit: float32 [128], P('members'), parts along dimension 0, may hold values from -12 to 12
Outputs:
- sat_adjoint: float32 [32, 64, 512], P(('members', 'layer'), 'areal'), parts along dimension 0
- pressure_adjoint: float32 [32, 64, 512], P(('members', 'layer'), 'areal'), parts along dimension 0
There are 2 independent parts, one for each index of `members`. A program takes and returns all parts, laid end to end along the dimension named above; each array names one. Nothing has to cross between parts.
Inputs may be any that keep to these rules, and one draw needn't show every extreme that they name: `cell_flags`: bits 0, 1, 2: the cell is upwind on its upper face along z, x, y; bit 3: the cell is active. `well_cells`: index (z * 64 + x) * 512 + y of the well's cell; wells may share a cell.
All inputs are finite; a program needn't handle non-finite values.
Results may differ from a plain program's by a relative error of at most 0.0001.
Values sent between devices are 32-bit elements; how exact they have to be, the bound alone decides.
A program may use at most 64 MiB of HBM per device.

v0:
```python
import functools

import jax
import jax.numpy as jnp
from jax import lax
from jax.experimental import pallas as pl
from jax.experimental.pallas import tpu as pltpu
from jax.sharding import PartitionSpec as P

ITERS = 4
MOBILITY_RATIO = 0.5
LOW_GROUP = 8
MESH = pl.DeviceIdType.MESH


def flow_fraction(wetness):
    square = wetness * wetness
    dry = 1.0 - wetness
    inverse = 1.0 / (square + MOBILITY_RATIO * (dry * dry))
    return square * inverse, (2.0 * MOBILITY_RATIO) * wetness * dry * (inverse * inverse)


def face_terms(face, scaled, press, frac, slope, upwind):
    moved = face * (scaled[1] - scaled[0])
    push = moved * jnp.where(upwind, frac[0], frac[1])
    drive = moved * (press[0] - press[1]) * jnp.where(upwind, slope[0], slope[1])
    return push, jnp.where(upwind, drive, 0.0), jnp.where(upwind, 0.0, drive)


def galerkin(moments):
    def inner(i, j):
        return 0.5 * (moments[i + j] + moments[abs(i - j)])

    def entry(i, j):
        moved = inner(i, 1) if j == 0 else 0.5 * (inner(i, j + 1) + inner(i, j - 1))
        return inner(i, j) - moved

    size = ITERS
    lower = [[None] * size for _ in range(size)]
    inverse = []
    forward = []
    for i in range(size):
        for j in range(i):
            total = entry(i, j)
            for k in range(j):
                total = total - lower[i][k] * lower[j][k] * inverse[k]
            lower[i][j] = total
        diagonal = entry(i, i)
        pivot = diagonal
        right = moments[i]
        for k in range(i):
            scale = lower[i][k] * inverse[k]
            pivot = pivot - scale * lower[i][k]
            right = right - scale * forward[k]
        keep = pivot > 1e-6 * diagonal
        inv = jnp.where(keep, 1.0 / jnp.where(keep, pivot, 1.0), 0.0)
        inverse.append(inv)
        forward.append(right)
    solved = [None] * size
    for i in range(size - 1, -1, -1):
        total = forward[i]
        for k in range(i + 1, size):
            total = total - lower[k][i] * solved[k]
        solved[i] = total * inverse[i]
    return solved


def kernel(
    areal_count,
    press_in, wet_in, cot_in, dt_in, comp_in, trans_in, flags_in, cells_in, misfit_in,
    sat_out, sol_out,
    press, wet, cot, dt, comp, trans, flags, cells, misfit,
    scaled, frac, slope, resid, sat_res, sol_res,
    face_z, inv_pivot, down_gain, up_gain,
    face_xu, face_xl, face_yu, face_yl, face_edge, face_zedge,
    basis, source,
    send_hi, send_lo, send_z, recv_hi, recv_lo, recv_z,
    vec_hi, vec_lo, got_hi, got_lo, got_z,
    sums, others,
    in_sem, out_sem, face_send, face_recv, vec_send, vec_recv, sum_send, sum_recv,
):
    depth, width, span = press.shape
    areal = lax.axis_index("areal")
    layer = lax.axis_index("layer")
    has_lo = areal > 0
    has_hi = areal < areal_count - 1
    lower_id = {"areal": jnp.maximum(areal - 1, 0), "layer": layer}
    upper_id = {"areal": jnp.minimum(areal + 1, areal_count - 1), "layer": layer}
    other_id = {"areal": areal, "layer": 1 - layer}
    edge = (depth - 1) * (1 - layer)

    low = min(LOW_GROUP, areal_count)
    high = areal_count // low
    place = lax.rem(areal, low)
    first = areal - place
    flat = place * 2 + layer
    stages = [[]]
    for step in range(1, 2 * low):
        peer = lax.rem(flat + step, 2 * low)
        stages[0].append({"areal": first + lax.div(peer, 2), "layer": lax.rem(peer, 2)})
    if high > 1:
        row = lax.div(areal, low)
        stages.append(
            [
                {"areal": lax.rem(row + step, high) * low + place, "layer": layer}
                for step in range(1, high)
            ]
        )

    pairs = [
        (cells_in, cells), (misfit_in, misfit), (cot_in, cot), (dt_in, dt), (flags_in, flags),
        (press_in, press), (wet_in, wet), (trans_in, trans), (comp_in, comp),
    ]
    loads = [
        pltpu.make_async_copy(src, dst, in_sem.at[place_of])
        for place_of, (src, dst) in enumerate(pairs)
    ]
    for load in loads:
        load.start()

    barrier = pltpu.get_barrier_semaphore()
    for stage in stages:
        for peer_id in stage:
            pl.semaphore_signal(barrier, inc=1, device_id=peer_id, device_id_type=MESH)
    expected = sum(len(stage) for stage in stages)
    if high > 1:
        @pl.when(has_lo)
        def _():
            pl.semaphore_signal(barrier, inc=1, device_id=lower_id, device_id_type=MESH)

        @pl.when(has_hi)
        def _():
            pl.semaphore_signal(barrier, inc=1, device_id=upper_id, device_id_type=MESH)

    @pl.when(jnp.logical_not(has_lo))
    def _():
        recv_lo[...] = jnp.zeros_like(recv_lo)
        got_lo[...] = jnp.zeros_like(got_lo)

    @pl.when(jnp.logical_not(has_hi))
    def _():
        recv_hi[...] = jnp.zeros_like(recv_hi)
        got_hi[...] = jnp.zeros_like(got_hi)

    rows = lax.broadcasted_iota(jnp.int32, (width, span), 0)
    lanes = lax.broadcasted_iota(jnp.int32, (width, span), 1)
    is_low_row = rows == 0
    is_high_row = rows == width - 1
    is_last_lane = lanes == span - 1

    def next_y(value):
        return pltpu.roll(value, span - 1, 1)

    def prev_y(value):
        return pltpu.roll(value, 1, 1)

    def next_x(value):
        return pltpu.roll(value, width - 1, 0)

    def prev_x(value):
        return pltpu.roll(value, 1, 0)

    loads[0].wait()
    loads[1].wait()
    cell = cells[...]
    wells = cell.shape[1]
    local = lax.broadcasted_iota(jnp.int32, (depth * width, wells), 0)
    base = (
        (layer * depth + lax.shift_right_logical(local, (width - 1).bit_length()))
        * (areal_count * width)
        + areal * width + lax.bitwise_and(local, width - 1)
    ) * span
    offset = cell - base
    by_row = jnp.where((offset >= 0) & (offset < span), misfit[...], 0.0)
    lane_of = lax.bitwise_and(cell, span - 1)
    by_lane = jnp.where(
        lax.broadcasted_iota(jnp.int32, (span, wells), 0) == lane_of, 1.0, 0.0
    )
    added = lax.dot_general(
        by_row, by_lane, (((1,), (1,)), ((), ())),
        precision=lax.Precision.HIGHEST, preferred_element_type=jnp.float32,
    )
    for load in loads[2:8]:
        load.wait()
    act = []
    for l in range(depth):
        modified = cot[l] + added[l * width : (l + 1) * width]
        sat_res[l] = modified
        scaled[l] = dt[l] * modified
        act.append(jnp.where((flags[l] & 8) != 0, 1.0, 0.0))

    for l in range(depth):
        here = slice(l, l + 1)
        top = slice(width - 1, width)
        live_x = trans[1, l] * act[l]
        up_x = jnp.where((flags[l] & 2) != 0, 1.0, 0.0)
        for k, plane in enumerate((press[l], scaled[l], wet[l], live_x, up_x)):
            send_hi[k, here] = plane[top]
        for k, plane in enumerate((press[l], scaled[l], wet[l], act[l])):
            send_lo[k, here] = plane[0:1]
    edge_act = jnp.where((flags[edge] & 8) != 0, 1.0, 0.0)
    send_z[0] = press[edge]
    send_z[1] = scaled[edge]
    send_z[2] = wet[edge]
    send_z[3] = edge_act
    send_z[4] = trans[0, edge] * edge_act
    send_z[5] = jnp.where((flags[edge] & 1) != 0, 1.0, 0.0)

    pl.semaphore_wait(barrier, expected)
    if high > 1:
        @pl.when(has_lo)
        def _():
            pl.semaphore_wait(barrier, 1)

        @pl.when(has_hi)
        def _():
            pl.semaphore_wait(barrier, 1)

    def remote(src, dst, send_sem, recv_sem, target):
        return pltpu.make_async_remote_copy(
            src_ref=src, dst_ref=dst, send_sem=send_sem, recv_sem=recv_sem,
            device_id=target, device_id_type=MESH,
        )

    def exchange(up_copy, low_copy, z_copy):
        z_copy.start()

        @pl.when(has_hi)
        def _():
            up_copy.start()

        @pl.when(has_lo)
        def _():
            low_copy.start()

    def arrived(up_copy, low_copy, z_copy):
        z_copy.wait_recv()

        @pl.when(has_lo)
        def _():
            up_copy.wait_recv()

        @pl.when(has_hi)
        def _():
            low_copy.wait_recv()

    def departed(up_copy, low_copy, z_copy):
        z_copy.wait_send()

        @pl.when(has_hi)
        def _():
            up_copy.wait_send()

        @pl.when(has_lo)
        def _():
            low_copy.wait_send()

    copies = [
        (
            remote(send_hi, recv_lo, face_send.at[0], face_recv.at[0], upper_id),
            remote(send_lo, recv_hi, face_send.at[1], face_recv.at[1], lower_id),
            remote(send_z, recv_z, face_send.at[2], face_recv.at[2], other_id),
        )
    ]
    exchange(*copies[0])

    for l in range(depth):
        share, rise = flow_fraction(wet[l])
        frac[l] = share
        slope[l] = rise
    carried = None
    for l in range(depth):
        up = (flags[l] & 4) != 0
        face = jnp.where(is_last_lane, 0.0, trans[2, l] * act[l] * next_y(act[l]))
        face_yu[l] = face
        face_yl[l] = prev_y(face)
        push, drive_here, drive_next = face_terms(
            face,
            (scaled[l], next_y(scaled[l])),
            (press[l], next_y(press[l])),
            (frac[l], next_y(frac[l])),
            (slope[l], next_y(slope[l])),
            up,
        )
        pushed = push - prev_y(push)
        driven = sat_res[l] + drive_here + prev_y(drive_next)
        if carried is not None:
            pushed = pushed - carried[0]
            driven = driven + carried[1]
        if l < depth - 1:
            face = trans[0, l] * act[l] * act[l + 1]
            face_z[l] = face
            push, drive_here, drive_next = face_terms(
                face,
                (scaled[l], scaled[l + 1]),
                (press[l], press[l + 1]),
                (frac[l], frac[l + 1]),
                (slope[l], slope[l + 1]),
                (flags[l] & 1) != 0,
            )
            pushed = pushed + push
            driven = driven + drive_here
            carried = (push, drive_next)
        resid[l] = pushed
        sat_res[l] = driven

    arrived(*copies[0])

    below = layer == 0
    z_share, z_rise = flow_fraction(recv_z[2])
    live = jnp.where(below, trans[0, edge] * edge_act * recv_z[3], recv_z[4] * edge_act)
    face_zedge[...] = live
    up_edge = jnp.where(below, send_z[5], recv_z[5]) > 0.5

    def ordered(mine, theirs):
        return jnp.where(below, mine, theirs), jnp.where(below, theirs, mine)

    push, drive_here, drive_next = face_terms(
        live,
        ordered(send_z[1], recv_z[1]),
        ordered(send_z[0], recv_z[0]),
        ordered(frac[edge], z_share),
        ordered(slope[edge], z_rise),
        up_edge,
    )
    resid[edge] = resid[edge] + jnp.where(below, push, -push)
    sat_res[edge] = sat_res[edge] + jnp.where(below, drive_here, drive_next)

    hi_share, hi_rise = flow_fraction(recv_hi[2])
    lo_share, lo_rise = flow_fraction(recv_lo[2])
    own_share, own_rise = flow_fraction(send_lo[2])
    low_face = recv_lo[3] * send_lo[3]
    low_push, _, low_drive = face_terms(
        low_face,
        (recv_lo[1], send_lo[1]),
        (recv_lo[0], send_lo[0]),
        (lo_share, own_share),
        (lo_rise, own_rise),
        recv_lo[4] > 0.5,
    )
    hi_press, hi_scaled, hi_act = recv_hi[0], recv_hi[1], recv_hi[3]

    def with_high(value, plane, l):
        return jnp.where(is_high_row, plane[l : l + 1], next_x(value))

    def with_low(value, plane, l):
        return jnp.where(is_low_row, plane[l : l + 1], prev_x(value))

    loads[8].wait()
    for l in range(depth):
        face = trans[1, l] * act[l] * with_high(act[l], hi_act, l)
        push, drive_here, drive_next = face_terms(
            face,
            (scaled[l], with_high(scaled[l], hi_scaled, l)),
            (press[l], with_high(press[l], hi_press, l)),
            (frac[l], with_high(frac[l], hi_share, l)),
            (slope[l], with_high(slope[l], hi_rise, l)),
            (flags[l] & 2) != 0,
        )
        resid[l] = resid[l] + push - with_low(push, low_push, l)
        sat_res[l] = sat_res[l] + drive_here + with_low(drive_next, low_drive, l)
        face_low = with_low(face, low_face, l)
        face_xu[l] = jnp.where(is_high_row, 0.0, face)
        face_xl[l] = jnp.where(is_low_row, 0.0, face_low)
        face_edge[l] = jnp.where(
            is_high_row, face, jnp.where(is_low_row, face_low, 0.0)
        )
        diagonal = comp[l] + face + face_low + face_yu[l] + face_yl[l]
        if l > 0:
            diagonal = diagonal + face_z[l - 1]
        else:
            diagonal = diagonal + jnp.where(below, 0.0, live)
        if l < depth - 1:
            diagonal = diagonal + face_z[l]
        else:
            diagonal = diagonal + jnp.where(below, live, 0.0)
        pivot = diagonal if l == 0 else diagonal - face_z[l - 1] * up_gain[l - 1]
        inverse = 1.0 / pivot
        inv_pivot[l] = inverse
        if l > 0:
            down_gain[l] = face_z[l - 1] * inverse
        if l < depth - 1:
            up_gain[l] = face_z[l] * inverse

    store_sat = pltpu.make_async_copy(sat_res, sat_out, out_sem.at[0])
    store_sat.start()

    def moment(left, right):
        total = None
        for l in range(depth):
            term = left[l] * right[l]
            total = term if total is None else total + term
        return total

    def fold(plane):
        total = plane[:, 0:128]
        for start in range(128, span, 128):
            total = total + plane[:, start : start + 128]
        return jnp.sum(total, axis=0, keepdims=True)

    older = None
    current = [resid[l] for l in range(depth)]
    products = []
    for step in range(ITERS):
        partial = [current[0] * inv_pivot[0]]
        for l in range(1, depth):
            partial.append(current[l] * inv_pivot[l] + down_gain[l] * partial[l - 1])
        vector = [None] * depth
        vector[depth - 1] = partial[depth - 1]
        for l in range(depth - 2, -1, -1):
            vector[l] = partial[l] + up_gain[l] * vector[l + 1]
        for l in range(depth):
            basis[step, l] = vector[l]
            vec_hi[step, l : l + 1] = vector[l][width - 1 : width]
            vec_lo[step, l : l + 1] = vector[l][0:1]
        tags = [3 * step + k for k in range(3)]
        trio = (
            remote(
                vec_hi.at[step], got_lo.at[step],
                vec_send.at[tags[0]], vec_recv.at[tags[0]], upper_id,
            ),
            remote(
                vec_lo.at[step], got_hi.at[step],
                vec_send.at[tags[1]], vec_recv.at[tags[1]], lower_id,
            ),
            remote(
                basis.at[step, edge], got_z.at[step],
                vec_send.at[tags[2]], vec_recv.at[tags[2]], other_id,
            ),
        )
        copies.append(trio)
        exchange(*trio)
        products.append(fold(moment(vector, current)))
        for l in range(depth):
            near = (
                face_xu[l] * next_x(vector[l])
                + face_xl[l] * prev_x(vector[l])
                + face_yu[l] * next_y(vector[l])
                + face_yl[l] * prev_y(vector[l])
            )
            source[l] = near
        arrived(*trio)
        source[edge] = source[edge] + face_zedge[...] * got_z[step]
        later = []
        for l in range(depth):
            halo = jnp.where(
                rows < width // 2, got_lo[step, l : l + 1], got_hi[step, l : l + 1]
            )
            value = source[l] + face_edge[l] * halo
            if step > 0:
                value = 2.0 * value - older[l]
            later.append(value)
        products.append(fold(moment(vector, later)))
        older, current = current, later

    for k, value in enumerate(products):
        sums[0, k : k + 1] = value
    sends = []
    slot = 0
    for place_of, stage in enumerate(stages):
        batch = [
            remote(
                sums.at[place_of], others.at[slot + k],
                sum_send.at[slot + k], sum_recv.at[slot + k], peer_id,
            )
            for k, peer_id in enumerate(stage)
        ]
        for copy in batch:
            copy.start()
        total = sums[place_of]
        for k, copy in enumerate(batch):
            copy.wait_recv()
        for k in range(len(batch)):
            total = total + others[slot + k]
        if place_of + 1 < len(stages):
            sums[place_of + 1] = total
        sends += batch
        slot += len(batch)
    total = jnp.sum(total, axis=1, keepdims=True)
    raw = [total[k : k + 1] for k in range(2 * ITERS)]
    moments = [raw[0], raw[1]]
    for k in range(2, 2 * ITERS):
        moments.append(2.0 * raw[k] - raw[k % 2])
    weights = [jnp.broadcast_to(value, (width, span)) for value in galerkin(moments)]
    for l in range(depth):
        value = weights[0] * basis[0, l]
        for step in range(1, ITERS):
            value = value + weights[step] * basis[step, l]
        sol_res[l] = value
    store_sol = pltpu.make_async_copy(sol_res, sol_out, out_sem.at[1])
    store_sol.start()
    for trio in copies:
        departed(*trio)
    for copy in sends:
        copy.wait_send()
    store_sat.wait()
    store_sol.wait()


def on_device(areal_count, *arrays):
    arrays = list(arrays)
    block = arrays[0].shape
    depth, width, span = block
    wells = arrays[7].shape[0]
    arrays[7] = arrays[7].reshape(1, wells)
    arrays[8] = arrays[8].reshape(1, wells)
    plane = (width, span)
    strip = (depth, span)
    low = min(LOW_GROUP, areal_count)
    slots = 2 * low - 1 + (areal_count // low - 1)
    f32 = jnp.float32
    cube = pltpu.VMEM(block, f32)

    def vmem(*shape):
        return pltpu.VMEM(shape, f32)

    scratch = [
        cube, cube, cube, cube, cube, vmem(3, *block), pltpu.VMEM(block, jnp.int32),
        pltpu.VMEM((1, wells), jnp.int32), vmem(1, wells),
        cube, cube, cube, cube, cube, cube,
        cube, cube, cube, cube,
        cube, cube, cube, cube, cube, vmem(*plane),
        vmem(ITERS, *block), cube,
        vmem(5, *strip), vmem(4, *strip), vmem(6, *plane),
        vmem(4, *strip), vmem(5, *strip), vmem(6, *plane),
        vmem(ITERS, *strip), vmem(ITERS, *strip),
        vmem(ITERS, *strip), vmem(ITERS, *strip), vmem(ITERS, *plane),
        vmem(2, 2 * ITERS, 128), vmem(slots, 2 * ITERS, 128),
        pltpu.SemaphoreType.DMA((9,)), pltpu.SemaphoreType.DMA((2,)),
        pltpu.SemaphoreType.DMA((3,)), pltpu.SemaphoreType.DMA((3,)),
        pltpu.SemaphoreType.DMA((3 * ITERS,)), pltpu.SemaphoreType.DMA((3 * ITERS,)),
        pltpu.SemaphoreType.DMA((slots,)), pltpu.SemaphoreType.DMA((slots,)),
    ]
    return pl.pallas_call(
        functools.partial(kernel, areal_count),
        out_shape=(jax.ShapeDtypeStruct(block, f32), jax.ShapeDtypeStruct(block, f32)),
        in_specs=[pl.BlockSpec(memory_space=pl.ANY)] * len(arrays),
        out_specs=(pl.BlockSpec(memory_space=pl.ANY), pl.BlockSpec(memory_space=pl.ANY)),
        scratch_shapes=scratch,
        compiler_params=pltpu.CompilerParams(
            collective_id=0, has_side_effects=True, vmem_limit_bytes=32 * 1024 * 1024
        ),
    )(*arrays)


def solution(mesh):
    block = P(("members", "layer"), "areal", None)
    return jax.shard_map(
        functools.partial(on_device, mesh.shape["areal"]),
        mesh=mesh,
        in_specs=(
            block, block, block, block, block,
            P(None, ("members", "layer"), "areal", None),
            block, P("members"), P("members"),
        ),
        out_specs=(block, block),
        check_vma=False,
    )
```

profile of v0, /device:TPU:0, one launch (start us, length us, event | category | flops | bytes accessed | tf_op | source)
XLA Modules:
  0.0 39.3 jit_solution(7015431058430460688)
XLA Ops:
  0.6 0.0 copy-start.7
  0.6 0.0 copy-start.8
  0.7 0.6 %copy-done.7 = s32[64]{0:T(128)S(1)} copy-done((s32[64]{0:T(128)S(1)}, s32[64]{0:T(128)}, u32[]{:S(2)}) %copy-start.7) | copy-done | bytes 280
  1.3 0.0 copy-done.8
  1.3 0.0 copy-start
  1.3 1.0 %copy-done = f32[3,8,8,512]{3,2,1,0:T(8,128)S(1)} copy-done((f32[3,8,8,512]{3,2,1,0:T(8,128)S(1)}, f32[3,8,8,512]{3,2,1,0:T(8,128)}, u32[]{:S(2)}) %copy-start) | copy-done | bytes 393240
  2.3 0.0 copy-start.1
  2.3 0.9 %copy-done.1 = f32[8,8,512]{2,1,0:T(8,128)S(1)} copy-done((f32[8,8,512]{2,1,0:T(8,128)S(1)}, f32[8,8,512]{2,1,0:T(8,128)}, u32[]{:S(2)}) %copy-start.1) | copy-done | bytes 131096
  3.2 0.0 copy-start.2
  3.2 0.9 %copy-done.2 = f32[8,8,512]{2,1,0:T(8,128)S(1)} copy-done((f32[8,8,512]{2,1,0:T(8,128)S(1)}, f32[8,8,512]{2,1,0:T(8,128)}, u32[]{:S(2)}) %copy-start.2) | copy-done | bytes 131096
  4.1 0.0 copy-start.3
  4.1 0.9 %copy-done.3 = f32[8,8,512]{2,1,0:T(8,128)S(1)} copy-done((f32[8,8,512]{2,1,0:T(8,128)S(1)}, f32[8,8,512]{2,1,0:T(8,128)}, u32[]{:S(2)}) %copy-start.3) | copy-done | bytes 131096
  5.0 0.0 copy-start.4
  5.0 0.9 %copy-done.4 = f32[8,8,512]{2,1,0:T(8,128)S(1)} copy-done((f32[8,8,512]{2,1,0:T(8,128)S(1)}, f32[8,8,512]{2,1,0:T(8,128)}, u32[]{:S(2)}) %copy-start.4) | copy-done | bytes 131096
  5.9 0.0 copy-start.5
  5.9 0.9 %copy-done.5 = f32[8,8,512]{2,1,0:T(8,128)S(1)} copy-done((f32[8,8,512]{2,1,0:T(8,128)S(1)}, f32[8,8,512]{2,1,0:T(8,128)}, u32[]{:S(2)}) %copy-start.5) | copy-done | bytes 131096
  6.8 0.0 copy-start.6
  6.8 0.9 %copy-done.6 = s32[8,8,512]{2,1,0:T(8,128)S(1)} copy-done((s32[8,8,512]{2,1,0:T(8,128)S(1)}, s32[8,8,512]{2,1,0:T(8,128)}, u32[]{:S(2)}) %copy-start.6) | copy-done | bytes 131096
  7.7 30.3 %shard_map.104 = (f32[8,8,512]{2,1,0:T(8,128)S(1)}, f32[8,8,512]{2,1,0:T(8,128)S(1)}) custom-call(f32[8,8,512]{2,1,0:T(8,128)S(1)} %copy-done.1, f32[8,8,512]{2,1,0:T(8,128)S(1)} %copy-done.2, f32[8,8,512]{2,1,0:T(8,128)S(1)} %copy-done.3, f32[8,8,512]{2,1,0:T(8,128)S(1)} %copy-done.4, f32[8,8,512]{2,1,0:T(8,128)S(1)} %copy-done.5, ...), custom_call_target="tpu_custom_call" | custom-call | tf_op jit(solution)/shard_map/pallas_call | solution.py:534
  38.0 0.7 %copy.13 = f32[8,8,512]{2,1,0:T(8,128)} copy(f32[8,8,512]{2,1,0:T(8,128)S(1)} %get-tuple-element.4) | data formatting | bytes 262144
  38.7 0.7 %copy.14 = f32[8,8,512]{2,1,0:T(8,128)} copy(f32[8,8,512]{2,1,0:T(8,128)S(1)} %get-tuple-element.5) | data formatting | bytes 262144
Async XLA Ops:
  0.6 0.7 %copy-start.7 = (s32[64]{0:T(128)S(1)}, s32[64]{0:T(128)}, u32[]{:S(2)}) copy-start(s32[64]{0:T(128)} %param.16) | copy-start | bytes 772
  0.6 0.7 %copy-start.8 = (f32[64]{0:T(128)S(1)}, f32[64]{0:T(128)}, u32[]{:S(2)}) copy-start(f32[64]{0:T(128)} %param.17) | copy-start | bytes 772
  1.3 1.0 %copy-start = (f32[3,8,8,512]{3,2,1,0:T(8,128)S(1)}, f32[3,8,8,512]{3,2,1,0:T(8,128)}, u32[]{:S(2)}) copy-start(f32[3,8,8,512]{3,2,1,0:T(8,128)} %trans_in.1) | copy-start | bytes 1179652
  2.3 0.9 %copy-start.1 = (f32[8,8,512]{2,1,0:T(8,128)S(1)}, f32[8,8,512]{2,1,0:T(8,128)}, u32[]{:S(2)}) copy-start(f32[8,8,512]{2,1,0:T(8,128)} %press_in.1) | copy-start | bytes 393220
  3.2 0.9 %copy-start.2 = (f32[8,8,512]{2,1,0:T(8,128)S(1)}, f32[8,8,512]{2,1,0:T(8,128)}, u32[]{:S(2)}) copy-start(f32[8,8,512]{2,1,0:T(8,128)} %wet_in.1) | copy-start | bytes 393220
  4.1 0.9 %copy-start.3 = (f32[8,8,512]{2,1,0:T(8,128)S(1)}, f32[8,8,512]{2,1,0:T(8,128)}, u32[]{:S(2)}) copy-start(f32[8,8,512]{2,1,0:T(8,128)} %cot_in.1) | copy-start | bytes 393220
  5.0 0.9 %copy-start.4 = (f32[8,8,512]{2,1,0:T(8,128)S(1)}, f32[8,8,512]{2,1,0:T(8,128)}, u32[]{:S(2)}) copy-start(f32[8,8,512]{2,1,0:T(8,128)} %dt_in.1) | copy-start | bytes 393220
  5.9 0.9 %copy-start.5 = (f32[8,8,512]{2,1,0:T(8,128)S(1)}, f32[8,8,512]{2,1,0:T(8,128)}, u32[]{:S(2)}) copy-start(f32[8,8,512]{2,1,0:T(8,128)} %comp_in.1) | copy-start | bytes 393220
  6.8 0.9 %copy-start.6 = (s32[8,8,512]{2,1,0:T(8,128)S(1)}, s32[8,8,512]{2,1,0:T(8,128)}, u32[]{:S(2)}) copy-start(s32[8,8,512]{2,1,0:T(8,128)} %flags_in.1) | copy-start | bytes 393220
where the time goes:
time: 39.6 us; the launch traced here: 39.3 us
  Pallas kernels  30.3 us (77%)
  local copies, waits for them, and re-layouts  8.39 us (21%)
  between operations  0.67 us (2%)
    pallas_call x1, Pallas kernels, on_device(): pl.pallas_call(functools.partial(kernel, areal_count), out_shape=(jax.Sha...  30.3 us
    unnamed x20, local copies, waits for them, and re-layouts  8.39 us

commit v1 on v0

--- a/solution.py
+++ b/solution.py
@@ -93,11 +93,13 @@
     high = areal_count // low
     place = lax.rem(areal, low)
     first = areal - place
-    flat = place * 2 + layer
-    stages = [[]]
-    for step in range(1, 2 * low):
-        peer = lax.rem(flat + step, 2 * low)
-        stages[0].append({"areal": first + lax.div(peer, 2), "layer": lax.rem(peer, 2)})
+    stages = [
+        [other_id],
+        [
+            {"areal": first + lax.rem(place + step, low), "layer": layer}
+            for step in range(1, low)
+        ],
+    ]
     if high > 1:
         row = lax.div(areal, low)
         stages.append(
@@ -507,7 +509,7 @@
     plane = (width, span)
     strip = (depth, span)
     low = min(LOW_GROUP, areal_count)
-    slots = 2 * low - 1 + (areal_count // low - 1)
+    slots = low + (areal_count // low - 1)
     f32 = jnp.float32
     cube = pltpu.VMEM(block, f32)
 
@@ -525,7 +527,7 @@
         vmem(4, *strip), vmem(5, *strip), vmem(6, *plane),
         vmem(ITERS, *strip), vmem(ITERS, *strip),
         vmem(ITERS, *strip), vmem(ITERS, *strip), vmem(ITERS, *plane),
-        vmem(2, 2 * ITERS, 128), vmem(slots, 2 * ITERS, 128),
+        vmem(3, 2 * ITERS, 128), vmem(slots, 2 * ITERS, 128),
         pltpu.SemaphoreType.DMA((9,)), pltpu.SemaphoreType.DMA((2,)),
         pltpu.SemaphoreType.DMA((3,)), pltpu.SemaphoreType.DMA((3,)),
         pltpu.SemaphoreType.DMA((3 * ITERS,)), pltpu.SemaphoreType.DMA((3 * ITERS,)),
@@ -538,7 +540,7 @@
         out_specs=(pl.BlockSpec(memory_space=pl.ANY), pl.BlockSpec(memory_space=pl.ANY)),
         scratch_shapes=scratch,
         compiler_params=pltpu.CompilerParams(
-            collective_id=0, has_side_effects=True, vmem_limit_bytes=32 * 1024 * 1024
+            collective_id=0, has_side_effects=True, vmem_limit_bytes=60 * 1024 * 1024
         ),
     )(*arrays)
 

time: 39.6 us -> 31.6 us (0.80)
  local copies, waits for them, and re-layouts: 8.39 us -> 2.26 us
  Pallas kernels: 30.3 us -> 28.5 us
    unnamed x20 -> x4, local copies, waits for them, and re-layouts: 8.39 us -> 2.26 us
    pallas_call x1, Pallas kernels: 30.3 us -> 28.5 us  [on_device(): pl.pallas_call(functools.partial(kernel, areal_count), out_shape=(jax.Sha...]
where the time goes in v1:
time: 31.6 us; the launch traced here: 31.4 us
  Pallas kernels  28.5 us (90%)
  local copies, waits for them, and re-layouts  2.26 us (7%)
  between operations  0.65 us (2%)
    pallas_call x1, Pallas kernels, on_device(): pl.pallas_call(functools.partial(kernel, areal_count), out_shape=(jax.Sha...  28.5 us
    unnamed x4, local copies, waits for them, and re-layouts  2.26 us

profile of v1, /device:TPU:0, one launch (start us, length us, event | category | flops | bytes accessed | tf_op | source)
XLA Modules:
  0.0 31.4 jit_solution(15775794664404714622)
XLA Ops:
  0.6 28.5 %shard_map.104 = (f32[8,8,512]{2,1,0:T(8,128)}, f32[8,8,512]{2,1,0:T(8,128)}) custom-call(f32[8,8,512]{2,1,0:T(8,128)} %press_in.1, f32[8,8,512]{2,1,0:T(8,128)} %wet_in.1, f32[8,8,512]{2,1,0:T(8,128)} %cot_in.1, f32[8,8,512]{2,1,0:T(8,128)} %dt_in.1, f32[8,8,512]{2,1,0:T(8,128)} %comp_in.1, f32[3,8,8,512]{3,2,1,0:T(8,128)} %trans_in.1, ...), custom_call_target="tpu_custom_call" | custom-call | tf_op jit(solution)/shard_map/pallas_call | solution.py:536
  29.1 0.0 copy-start
  29.1 1.6 %copy.13 = f32[8,8,512]{2,1,0:T(8,128)} copy(f32[8,8,512]{2,1,0:T(8,128)} %get-tuple-element.4) | data formatting | bytes 262144
  30.7 0.0 copy-done
  30.7 0.7 %copy.14 = f32[8,8,512]{2,1,0:T(8,128)} copy(f32[8,8,512]{2,1,0:T(8,128)S(1)} %copy-done) | data formatting | bytes 262144
Async XLA Ops:
  29.1 1.6 %copy-start = (f32[8,8,512]{2,1,0:T(8,128)S(1)}, f32[8,8,512]{2,1,0:T(8,128)}, u32[]{:S(2)}) copy-start(f32[8,8,512]{2,1,0:T(8,128)} %get-tuple-element.5) | copy-start | bytes 393220

commit v2 on v1

--- a/solution.py
+++ b/solution.py
@@ -76,6 +76,8 @@
     basis, source,
     send_hi, send_lo, send_z, recv_hi, recv_lo, recv_z,
     vec_hi, vec_lo, got_hi, got_lo, got_z,
+    coef_hi, coef_lo, got_coef_hi, got_coef_lo, edge_face,
+    diag_hi, diag_lo, got_diag_hi, got_diag_lo,
     sums, others,
     in_sem, out_sem, face_send, face_recv, vec_send, vec_recv, sum_send, sum_recv,
 ):
@@ -87,6 +89,8 @@
     lower_id = {"areal": jnp.maximum(areal - 1, 0), "layer": layer}
     upper_id = {"areal": jnp.minimum(areal + 1, areal_count - 1), "layer": layer}
     other_id = {"areal": areal, "layer": 1 - layer}
+    lower_diag = {"areal": jnp.maximum(areal - 1, 0), "layer": 1 - layer}
+    upper_diag = {"areal": jnp.minimum(areal + 1, areal_count - 1), "layer": 1 - layer}
     edge = (depth - 1) * (1 - layer)
 
     low = min(LOW_GROUP, areal_count)
@@ -125,30 +129,38 @@
         for peer_id in stage:
             pl.semaphore_signal(barrier, inc=1, device_id=peer_id, device_id_type=MESH)
     expected = sum(len(stage) for stage in stages)
-    if high > 1:
-        @pl.when(has_lo)
-        def _():
-            pl.semaphore_signal(barrier, inc=1, device_id=lower_id, device_id_type=MESH)
-
-        @pl.when(has_hi)
-        def _():
-            pl.semaphore_signal(barrier, inc=1, device_id=upper_id, device_id_type=MESH)
+    beside = 2 if high > 1 else 1
+
+    @pl.when(has_lo)
+    def _():
+        for peer_id in (lower_diag, lower_id)[:beside]:
+            pl.semaphore_signal(barrier, inc=1, device_id=peer_id, device_id_type=MESH)
+
+    @pl.when(has_hi)
+    def _():
+        for peer_id in (upper_diag, upper_id)[:beside]:
+            pl.semaphore_signal(barrier, inc=1, device_id=peer_id, device_id_type=MESH)
 
     @pl.when(jnp.logical_not(has_lo))
     def _():
         recv_lo[...] = jnp.zeros_like(recv_lo)
         got_lo[...] = jnp.zeros_like(got_lo)
+        got_coef_lo[...] = jnp.zeros_like(got_coef_lo)
+        got_diag_lo[...] = jnp.zeros_like(got_diag_lo)
 
     @pl.when(jnp.logical_not(has_hi))
     def _():
         recv_hi[...] = jnp.zeros_like(recv_hi)
         got_hi[...] = jnp.zeros_like(got_hi)
+        got_coef_hi[...] = jnp.zeros_like(got_coef_hi)
+        got_diag_hi[...] = jnp.zeros_like(got_diag_hi)
 
     rows = lax.broadcasted_iota(jnp.int32, (width, span), 0)
     lanes = lax.broadcasted_iota(jnp.int32, (width, span), 1)
     is_low_row = rows == 0
     is_high_row = rows == width - 1
     is_last_lane = lanes == span - 1
+    strip_rows = lax.broadcasted_iota(jnp.int32, (depth, span), 0)
 
     def next_y(value):
         return pltpu.roll(value, span - 1, 1)
@@ -208,15 +220,8 @@
     send_z[4] = trans[0, edge] * edge_act
     send_z[5] = jnp.where((flags[edge] & 1) != 0, 1.0, 0.0)
 
-    pl.semaphore_wait(barrier, expected)
-    if high > 1:
-        @pl.when(has_lo)
-        def _():
-            pl.semaphore_wait(barrier, 1)
-
-        @pl.when(has_hi)
-        def _():
-            pl.semaphore_wait(barrier, 1)
+    sides_there = jnp.where(has_lo, 1, 0) + jnp.where(has_hi, 1, 0)
+    pl.semaphore_wait(barrier, expected + beside * sides_there)
 
     def remote(src, dst, send_sem, recv_sem, target):
         return pltpu.make_async_remote_copy(
@@ -224,44 +229,54 @@
             device_id=target, device_id_type=MESH,
         )
 
-    def exchange(up_copy, low_copy, z_copy):
-        z_copy.start()
-
-        @pl.when(has_hi)
-        def _():
-            up_copy.start()
-
-        @pl.when(has_lo)
-        def _():
-            low_copy.start()
-
-    def arrived(up_copy, low_copy, z_copy):
-        z_copy.wait_recv()
-
-        @pl.when(has_lo)
-        def _():
-            up_copy.wait_recv()
-
-        @pl.when(has_hi)
-        def _():
-            low_copy.wait_recv()
-
-    def departed(up_copy, low_copy, z_copy):
-        z_copy.wait_send()
-
-        @pl.when(has_hi)
-        def _():
-            up_copy.wait_send()
-
-        @pl.when(has_lo)
-        def _():
-            low_copy.wait_send()
+    def exchange(ups, lows, across):
+        if ups:
+            @pl.when(has_hi)
+            def _():
+                for copy in ups:
+                    copy.start()
+
+            @pl.when(has_lo)
+            def _():
+                for copy in lows:
+                    copy.start()
+
+        for copy in across:
+            copy.start()
+
+    def arrived(ups, lows, across):
+        for copy in across:
+            copy.wait_recv()
+        if ups:
+            @pl.when(has_lo)
+            def _():
+                for copy in ups:
+                    copy.wait_recv()
+
+            @pl.when(has_hi)
+            def _():
+                for copy in lows:
+                    copy.wait_recv()
+
+    def departed(ups, lows, across):
+        for copy in across:
+            copy.wait_send()
+        if ups:
+            @pl.when(has_hi)
+            def _():
+                for copy in ups:
+                    copy.wait_send()
+
+            @pl.when(has_lo)
+            def _():
+                for copy in lows:
+                    copy.wait_send()
 
     copies = [
         (
-            remote(send_hi, recv_lo, face_send.at[0], face_recv.at[0], upper_id),
-            remote(send_lo, recv_hi, face_send.at[1], face_recv.at[1], lower_id),
-            remote(send_z, recv_z, face_send.at[2], face_recv.at[2], other_id),
+            [remote(send_hi, recv_lo, face_send.at[0], face_recv.at[0], upper_id)],
+            [remote(send_lo, recv_hi, face_send.at[1], face_recv.at[1], lower_id)],
+            [remote(send_z, recv_z, face_send.at[2], face_recv.at[2], other_id)],
         )
     ]
     exchange(*copies[0])
@@ -383,6 +398,13 @@
             down_gain[l] = face_z[l - 1] * inverse
         if l < depth - 1:
             up_gain[l] = face_z[l] * inverse
+        here = slice(l, l + 1)
+        joint = face_z[l] if l < depth - 1 else live
+        edge_face[here] = face[width - 1 : width]
+        for k, plane in enumerate((face_low, face_yu[l], inverse, joint)):
+            coef_hi[k, here] = plane[width - 1 : width]
+        for k, plane in enumerate((face, face_yu[l], inverse, joint)):
+            coef_lo[k, here] = plane[0:1]
 
     store_sat = pltpu.make_async_copy(sat_res, sat_out, out_sem.at[0])
     store_sat.start()
@@ -411,27 +433,46 @@
         vector[depth - 1] = partial[depth - 1]
         for l in range(depth - 2, -1, -1):
             vector[l] = partial[l] + up_gain[l] * vector[l + 1]
+        wide = step % 2 == 0
         for l in range(depth):
             basis[step, l] = vector[l]
-            vec_hi[step, l : l + 1] = vector[l][width - 1 : width]
-            vec_lo[step, l : l + 1] = vector[l][0:1]
-        tags = [3 * step + k for k in range(3)]
-        trio = (
-            remote(
-                vec_hi.at[step], got_lo.at[step],
-                vec_send.at[tags[0]], vec_recv.at[tags[0]], upper_id,
-            ),
-            remote(
-                vec_lo.at[step], got_hi.at[step],
-                vec_send.at[tags[1]], vec_recv.at[tags[1]], lower_id,
-            ),
-            remote(
-                basis.at[step, edge], got_z.at[step],
-                vec_send.at[tags[2]], vec_recv.at[tags[2]], other_id,
-            ),
-        )
+            if wide:
+                here = slice(l, l + 1)
+                vec_hi[step, 0, here] = vector[l][width - 1 : width]
+                vec_hi[step, 1, here] = vector[l][width - 2 : width - 1]
+                vec_lo[step, 0, here] = vector[l][0:1]
+                vec_lo[step, 1, here] = vector[l][1:2]
+        tag = 8 * step
+
+        def hop(src, dst, target):
+            nonlocal tag
+            tag += 1
+            return remote(src, dst, vec_send.at[tag - 1], vec_recv.at[tag - 1], target)
+
+        ups, lows = [], []
+        if wide:
+            outer = basis[step, edge]
+            diag_hi[step] = outer[width - 1 : width]
+            diag_lo[step] = outer[0:1]
+            ups = [
+                hop(vec_hi.at[step], got_lo.at[step], upper_id),
+                hop(diag_hi.at[step], got_diag_lo.at[step], upper_diag),
+            ]
+            lows = [
+                hop(vec_lo.at[step], got_hi.at[step], lower_id),
+                hop(diag_lo.at[step], got_diag_hi.at[step], lower_diag),
+            ]
+        trio = (ups, lows, [hop(basis.at[step, edge], got_z.at[step], other_id)])
         copies.append(trio)
         exchange(*trio)
+        if step == 0:
+            coefs = (
+                [hop(coef_hi, got_coef_lo, upper_id)],
+                [hop(coef_lo, got_coef_hi, lower_id)],
+                [],
+            )
+            copies.append(coefs)
+            exchange(*coefs)
         products.append(fold(moment(vector, current)))
         for l in range(depth):
             near = (
@@ -446,13 +487,46 @@
         later = []
         for l in range(depth):
             halo = jnp.where(
-                rows < width // 2, got_lo[step, l : l + 1], got_hi[step, l : l + 1]
+                rows < width // 2, got_lo[step, 0, l : l + 1], got_hi[step, 0, l : l + 1]
             )
             value = source[l] + face_edge[l] * halo
             if step > 0:
                 value = 2.0 * value - older[l]
             later.append(value)
         products.append(fold(moment(vector, later)))
+        if wide:
+            if step == 0:
+                arrived(*coefs)
+                halo_old = [None, None]
+            sides = (
+                (got_lo, vec_lo, got_coef_lo, got_diag_lo, recv_lo[3] * send_lo[3]),
+                (got_hi, vec_hi, got_coef_hi, got_diag_hi, edge_face[...]),
+            )
+            for side, (got, own, coef, diag, between) in enumerate(sides):
+                beside_it = got[step, 0]
+                value = (
+                    coef[0] * got[step, 1]
+                    + between * own[step, 0]
+                    + coef[1] * next_y(beside_it)
+                    + prev_y(coef[1] * beside_it)
+                )
+                joint = coef[3, depth - 1 : depth]
+                value = value + jnp.where(strip_rows == edge, joint * diag[step], 0.0)
+                if step > 0:
+                    value = 2.0 * value - halo_old[side]
+                halo_old[side] = value
+                inverse = coef[2]
+                scaled_value = value * inverse
+                gain_up = coef[3] * inverse
+                part = [scaled_value[0:1]]
+                for l in range(1, depth):
+                    gain = coef[3, l - 1 : l] * inverse[l : l + 1]
+                    part.append(scaled_value[l : l + 1] + gain * part[l - 1])
+                solved = part[depth - 1]
+                got[step + 1, 0, depth - 1 : depth] = solved
+                for l in range(depth - 2, -1, -1):
+                    solved = part[l] + gain_up[l : l + 1] * solved
+                    got[step + 1, 0, l : l + 1] = solved
         older, current = current, later
 
     for k, value in enumerate(products):
@@ -525,12 +599,14 @@
         vmem(ITERS, *block), cube,
         vmem(5, *strip), vmem(4, *strip), vmem(6, *plane),
         vmem(4, *strip), vmem(5, *strip), vmem(6, *plane),
-        vmem(ITERS, *strip), vmem(ITERS, *strip),
-        vmem(ITERS, *strip), vmem(ITERS, *strip), vmem(ITERS, *plane),
+        vmem(ITERS, 2, *strip), vmem(ITERS, 2, *strip),
+        vmem(ITERS, 2, *strip), vmem(ITERS, 2, *strip), vmem(ITERS, *plane),
+        vmem(4, *strip), vmem(4, *strip), vmem(4, *strip), vmem(4, *strip), vmem(*strip),
+        vmem(ITERS, 1, span), vmem(ITERS, 1, span), vmem(ITERS, 1, span), vmem(ITERS, 1, span),
         vmem(3, 2 * ITERS, 128), vmem(slots, 2 * ITERS, 128),
         pltpu.SemaphoreType.DMA((9,)), pltpu.SemaphoreType.DMA((2,)),
         pltpu.SemaphoreType.DMA((3,)), pltpu.SemaphoreType.DMA((3,)),
-        pltpu.SemaphoreType.DMA((3 * ITERS,)), pltpu.SemaphoreType.DMA((3 * ITERS,)),
+        pltpu.SemaphoreType.DMA((8 * ITERS,)), pltpu.SemaphoreType.DMA((8 * ITERS,)),
         pltpu.SemaphoreType.DMA((slots,)), pltpu.SemaphoreType.DMA((slots,)),
     ]
     return pl.pallas_call(

time: 31.6 us -> 31.1 us (0.984)
  Pallas kernels: 28.5 us -> 28 us
    pallas_call x1, Pallas kernels: 28.5 us -> 28 us  [on_device(): pl.pallas_call(functools.partial(kernel, areal_count), out_shape=(jax.Sha...]
where the time goes in v2:
time: 31.1 us; the launch traced here: 30.9 us
  Pallas kernels  28 us (90%)
  local copies, waits for them, and re-layouts  2.26 us (7%)
  between operations  0.65 us (2%)
    pallas_call x1, Pallas kernels, on_device(): pl.pallas_call(functools.partial(kernel, areal_count), out_shape=(jax.Sha...  28 us
    unnamed x4, local copies, waits for them, and re-layouts  2.26 us

profile of v2, /device:TPU:0, one launch (start us, length us, event | category | flops | bytes accessed | tf_op | source)
XLA Modules:
  0.0 30.9 jit_solution(17028718085685370524)
XLA Ops:
  0.6 28.0 %shard_map.104 = (f32[8,8,512]{2,1,0:T(8,128)}, f32[8,8,512]{2,1,0:T(8,128)}) custom-call(f32[8,8,512]{2,1,0:T(8,128)} %press_in.1, f32[8,8,512]{2,1,0:T(8,128)} %wet_in.1, f32[8,8,512]{2,1,0:T(8,128)} %cot_in.1, f32[8,8,512]{2,1,0:T(8,128)} %dt_in.1, f32[8,8,512]{2,1,0:T(8,128)} %comp_in.1, f32[3,8,8,512]{3,2,1,0:T(8,128)} %trans_in.1, ...), custom_call_target="tpu_custom_call" | custom-call | tf_op jit(solution)/shard_map/pallas_call | solution.py:612
  28.6 0.0 copy-start
  28.6 1.6 %copy.13 = f32[8,8,512]{2,1,0:T(8,128)} copy(f32[8,8,512]{2,1,0:T(8,128)} %get-tuple-element.4) | data formatting | bytes 262144
  30.2 0.0 copy-done
  30.2 0.7 %copy.14 = f32[8,8,512]{2,1,0:T(8,128)} copy(f32[8,8,512]{2,1,0:T(8,128)S(1)} %copy-done) | data formatting | bytes 262144
Async XLA Ops:
  28.6 1.6 %copy-start = (f32[8,8,512]{2,1,0:T(8,128)S(1)}, f32[8,8,512]{2,1,0:T(8,128)}, u32[]{:S(2)}) copy-start(f32[8,8,512]{2,1,0:T(8,128)} %get-tuple-element.5) | copy-start | bytes 393220

commit v3 on v2

--- a/solution.py
+++ b/solution.py
@@ -573,6 +573,17 @@
     store_sol.wait()
 
 
+def hand_over(sat_in, sol_in, sat_out, sol_out, sem):
+    moves = [
+        pltpu.make_async_copy(sat_in, sat_out, sem.at[0]),
+        pltpu.make_async_copy(sol_in, sol_out, sem.at[1]),
+    ]
+    for move in moves:
+        move.start()
+    for move in moves:
+        move.wait()
+
+
 def on_device(areal_count, *arrays):
     arrays = list(arrays)
     block = arrays[0].shape
@@ -609,7 +620,7 @@
         pltpu.SemaphoreType.DMA((8 * ITERS,)), pltpu.SemaphoreType.DMA((8 * ITERS,)),
         pltpu.SemaphoreType.DMA((slots,)), pltpu.SemaphoreType.DMA((slots,)),
     ]
-    return pl.pallas_call(
+    results = pl.pallas_call(
         functools.partial(kernel, areal_count),
         out_shape=(jax.ShapeDtypeStruct(block, f32), jax.ShapeDtypeStruct(block, f32)),
         in_specs=[pl.BlockSpec(memory_space=pl.ANY)] * len(arrays),
@@ -619,6 +630,13 @@
             collective_id=0, has_side_effects=True, vmem_limit_bytes=60 * 1024 * 1024
         ),
     )(*arrays)
+    return pl.pallas_call(
+        hand_over,
+        out_shape=(jax.ShapeDtypeStruct(block, f32), jax.ShapeDtypeStruct(block, f32)),
+        in_specs=[pl.BlockSpec(memory_space=pl.ANY)] * 2,
+        out_specs=(pl.BlockSpec(memory_space=pl.ANY), pl.BlockSpec(memory_space=pl.ANY)),
+        scratch_shapes=[pltpu.SemaphoreType.DMA((2,))],
+    )(*results)
 
 
 def solution(mesh):

time: 31.1 us -> 37.9 us (1.22)
  Pallas kernels: 28 us -> 37.1 us
  local copies, waits for them, and re-layouts: 2.26 us -> 0 us
    pallas_call x0 -> x1, Pallas kernels: none -> 9.06 us  [on_device(): pl.pallas_call(hand_over, out_shape=(jax.ShapeDtypeStruct(block, f32), ja...]
    unnamed x4 -> x0, local copies, waits for them, and re-layouts: 2.26 us -> none
where the time goes in v3:
time: 37.9 us; the launch traced here: 37.7 us
  Pallas kernels  37.1 us (98%)
  between operations  0.64 us (2%)
    pallas_call x1, Pallas kernels, on_device(): pl.pallas_call(functools.partial(kernel, areal_count), out_shape=(jax.Sha...  28 us
    pallas_call x1, Pallas kernels, on_device(): pl.pallas_call(hand_over, out_shape=(jax.ShapeDtypeStruct(block, f32), ja...  9.06 us

profile of v3, /device:TPU:0, one launch (start us, length us, event | category | flops | bytes accessed | tf_op | source)
XLA Modules:
  0.0 37.7 jit_solution(9881099676242203805)
XLA Ops:
  0.6 28.0 %shard_map.104 = (f32[8,8,512]{2,1,0:T(8,128)}, f32[8,8,512]{2,1,0:T(8,128)}) custom-call(f32[8,8,512]{2,1,0:T(8,128)} %press_in.1, f32[8,8,512]{2,1,0:T(8,128)} %wet_in.1, f32[8,8,512]{2,1,0:T(8,128)} %cot_in.1, f32[8,8,512]{2,1,0:T(8,128)} %dt_in.1, f32[8,8,512]{2,1,0:T(8,128)} %comp_in.1, f32[3,8,8,512]{3,2,1,0:T(8,128)} %trans_in.1, ...), custom_call_target="tpu_custom_call" | custom-call | tf_op jit(solution)/shard_map/pallas_call | solution.py:623
  28.6 9.1 %shard_map.105 = (f32[8,8,512]{2,1,0:T(8,128)}, f32[8,8,512]{2,1,0:T(8,128)}) custom-call(f32[8,8,512]{2,1,0:T(8,128)} %get-tuple-element.4.sat_in, f32[8,8,512]{2,1,0:T(8,128)} %get-tuple-element.5.sol_in), custom_call_target="tpu_custom_call" | custom-call | tf_op jit(solution)/shard_map/pallas_call | solution.py:633

commit v4 on v2

--- a/solution.py
+++ b/solution.py
@@ -422,6 +422,41 @@
             total = total + plane[:, start : start + 128]
         return jnp.sum(total, axis=0, keepdims=True)
 
+    halo_old = [None, None]
+
+    def advance_halo(step):
+            if step == 0:
+                arrived(*coefs)
+            sides = (
+                (got_lo, vec_lo, got_coef_lo, got_diag_lo, recv_lo[3] * send_lo[3]),
+                (got_hi, vec_hi, got_coef_hi, got_diag_hi, edge_face[...]),
+            )
+            for side, (got, own, coef, diag, between) in enumerate(sides):
+                beside_it = got[step, 0]
+                value = (
+                    coef[0] * got[step, 1]
+                    + between * own[step, 0]
+                    + coef[1] * next_y(beside_it)
+                    + prev_y(coef[1] * beside_it)
+                )
+                joint = coef[3, depth - 1 : depth]
+                value = value + jnp.where(strip_rows == edge, joint * diag[step], 0.0)
+                if step > 0:
+                    value = 2.0 * value - halo_old[side]
+                halo_old[side] = value
+                inverse = coef[2]
+                scaled_value = value * inverse
+                gain_up = coef[3] * inverse
+                part = [scaled_value[0:1]]
+                for l in range(1, depth):
+                    gain = coef[3, l - 1 : l] * inverse[l : l + 1]
+                    part.append(scaled_value[l : l + 1] + gain * part[l - 1])
+                solved = part[depth - 1]
+                got[step + 1, 0, depth - 1 : depth] = solved
+                for l in range(depth - 2, -1, -1):
+                    solved = part[l] + gain_up[l : l + 1] * solved
+                    got[step + 1, 0, l : l + 1] = solved
+
     older = None
     current = [resid[l] for l in range(depth)]
     products = []
@@ -483,6 +518,8 @@
             )
             source[l] = near
         arrived(*trio)
+        if not wide:
+            advance_halo(step - 1)
         source[edge] = source[edge] + face_zedge[...] * got_z[step]
         later = []
         for l in range(depth):
@@ -494,39 +531,6 @@
                 value = 2.0 * value - older[l]
             later.append(value)
         products.append(fold(moment(vector, later)))
-        if wide:
-            if step == 0:
-                arrived(*coefs)
-                halo_old = [None, None]
-            sides = (
-                (got_lo, vec_lo, got_coef_lo, got_diag_lo, recv_lo[3] * send_lo[3]),
-                (got_hi, vec_hi, got_coef_hi, got_diag_hi, edge_face[...]),
-            )
-            for side, (got, own, coef, diag, between) in enumerate(sides):
-                beside_it = got[step, 0]
-                value = (
-                    coef[0] * got[step, 1]
-                    + between * own[step, 0]
-                    + coef[1] * next_y(beside_it)
-                    + prev_y(coef[1] * beside_it)
-                )
-                joint = coef[3, depth - 1 : depth]
-                value = value + jnp.where(strip_rows == edge, joint * diag[step], 0.0)
-                if step > 0:
-                    value = 2.0 * value - halo_old[side]
-                halo_old[side] = value
-                inverse = coef[2]
-                scaled_value = value * inverse
-                gain_up = coef[3] * inverse
-                part = [scaled_value[0:1]]
-                for l in range(1, depth):
-                    gain = coef[3, l - 1 : l] * inverse[l : l + 1]
-                    part.append(scaled_value[l : l + 1] + gain * part[l - 1])
-                solved = part[depth - 1]
-                got[step + 1, 0, depth - 1 : depth] = solved
-                for l in range(depth - 2, -1, -1):
-                    solved = part[l] + gain_up[l : l + 1] * solved
-                    got[step + 1, 0, l : l + 1] = solved
         older, current = current, later
 
     for k, value in enumerate(products):

time: 31.1 us -> 30.5 us (0.981)
  Pallas kernels: 28 us -> 27.4 us
    pallas_call x1, Pallas kernels: 28 us -> 27.4 us  [on_device(): pl.pallas_call(functools.partial(kernel, areal_count), out_shape=(jax.Sha...]
where the time goes in v4:
time: 30.5 us; the launch traced here: 30.3 us
  Pallas kernels  27.4 us (90%)
  local copies, waits for them, and re-layouts  2.26 us (7%)
  between operations  0.65 us (2%)
    pallas_call x1, Pallas kernels, on_device(): pl.pallas_call(functools.partial(kernel, areal_count), out_shape=(jax.Sha...  27.4 us
    unnamed x4, local copies, waits for them, and re-layouts  2.26 us

profile of v4, /device:TPU:0, one launch (start us, length us, event | category | flops | bytes accessed | tf_op | source)
XLA Modules:
  0.0 30.3 jit_solution(11332251333597462459)
XLA Ops:
  0.6 27.4 %shard_map.104 = (f32[8,8,512]{2,1,0:T(8,128)}, f32[8,8,512]{2,1,0:T(8,128)}) custom-call(f32[8,8,512]{2,1,0:T(8,128)} %press_in.1, f32[8,8,512]{2,1,0:T(8,128)} %wet_in.1, f32[8,8,512]{2,1,0:T(8,128)} %cot_in.1, f32[8,8,512]{2,1,0:T(8,128)} %dt_in.1, f32[8,8,512]{2,1,0:T(8,128)} %comp_in.1, f32[3,8,8,512]{3,2,1,0:T(8,128)} %trans_in.1, ...), custom_call_target="tpu_custom_call" | custom-call | tf_op jit(solution)/shard_map/pallas_call | solution.py:616
  28.0 0.0 copy-start
  28.0 1.6 %copy.13 = f32[8,8,512]{2,1,0:T(8,128)} copy(f32[8,8,512]{2,1,0:T(8,128)} %get-tuple-element.4) | data formatting | bytes 262144
  29.6 0.0 copy-done
  29.6 0.7 %copy.14 = f32[8,8,512]{2,1,0:T(8,128)} copy(f32[8,8,512]{2,1,0:T(8,128)S(1)} %copy-done) | data formatting | bytes 262144
Async XLA Ops:
  28.0 1.6 %copy-start = (f32[8,8,512]{2,1,0:T(8,128)S(1)}, f32[8,8,512]{2,1,0:T(8,128)}, u32[]{:S(2)}) copy-start(f32[8,8,512]{2,1,0:T(8,128)} %get-tuple-element.5) | copy-start | bytes 393220

commit v5 on v4

--- a/solution.py
+++ b/solution.py
@@ -425,6 +425,7 @@
     halo_old = [None, None]
 
     def advance_halo(step):
+            arrived(*late)
             if step == 0:
                 arrived(*coefs)
             sides = (
@@ -477,7 +478,7 @@
                 vec_hi[step, 1, here] = vector[l][width - 2 : width - 1]
                 vec_lo[step, 0, here] = vector[l][0:1]
                 vec_lo[step, 1, here] = vector[l][1:2]
-        tag = 8 * step
+        tag = 10 * step
 
         def hop(src, dst, target):
             nonlocal tag
@@ -490,16 +491,28 @@
             diag_hi[step] = outer[width - 1 : width]
             diag_lo[step] = outer[0:1]
             ups = [
-                hop(vec_hi.at[step], got_lo.at[step], upper_id),
-                hop(diag_hi.at[step], got_diag_lo.at[step], upper_diag),
+                hop(vec_hi.at[step, 0], got_lo.at[step, 0], upper_id),
             ]
             lows = [
-                hop(vec_lo.at[step], got_hi.at[step], lower_id),
-                hop(diag_lo.at[step], got_diag_hi.at[step], lower_diag),
+                hop(vec_lo.at[step, 0], got_hi.at[step, 0], lower_id),
             ]
         trio = (ups, lows, [hop(basis.at[step, edge], got_z.at[step], other_id)])
         copies.append(trio)
         exchange(*trio)
+        if wide:
+            late = (
+                [
+                    hop(vec_hi.at[step, 1], got_lo.at[step, 1], upper_id),
+                    hop(diag_hi.at[step], got_diag_lo.at[step], upper_diag),
+                ],
+                [
+                    hop(vec_lo.at[step, 1], got_hi.at[step, 1], lower_id),
+                    hop(diag_lo.at[step], got_diag_hi.at[step], lower_diag),
+                ],
+                [],
+            )
+            copies.append(late)
+            exchange(*late)
         if step == 0:
             coefs = (
                 [hop(coef_hi, got_coef_lo, upper_id)],
@@ -610,7 +623,7 @@
         vmem(3, 2 * ITERS, 128), vmem(slots, 2 * ITERS, 128),
         pltpu.SemaphoreType.DMA((9,)), pltpu.SemaphoreType.DMA((2,)),
         pltpu.SemaphoreType.DMA((3,)), pltpu.SemaphoreType.DMA((3,)),
-        pltpu.SemaphoreType.DMA((8 * ITERS,)), pltpu.SemaphoreType.DMA((8 * ITERS,)),
+        pltpu.SemaphoreType.DMA((10 * ITERS,)), pltpu.SemaphoreType.DMA((10 * ITERS,)),
         pltpu.SemaphoreType.DMA((slots,)), pltpu.SemaphoreType.DMA((slots,)),
     ]
     return pl.pallas_call(

time: 30.5 us -> 30.3 us (level)
  no operation moved by 1% of the time
where the time goes in v5:
time: 30.3 us; the launch traced here: 30.2 us
  Pallas kernels  27.2 us (90%)
  local copies, waits for them, and re-layouts  2.26 us (7%)
  between operations  0.65 us (2%)
    pallas_call x1, Pallas kernels, on_device(): pl.pallas_call(functools.partial(kernel, areal_count), out_shape=(jax.Sha...  27.2 us
    unnamed x4, local copies, waits for them, and re-layouts  2.26 us

profile of v5, /device:TPU:0, one launch (start us, length us, event | category | flops | bytes accessed | tf_op | source)
XLA Modules:
  0.0 30.2 jit_solution(2287246801258378415)
XLA Ops:
  0.6 27.2 %shard_map.104 = (f32[8,8,512]{2,1,0:T(8,128)}, f32[8,8,512]{2,1,0:T(8,128)}) custom-call(f32[8,8,512]{2,1,0:T(8,128)} %press_in.1, f32[8,8,512]{2,1,0:T(8,128)} %wet_in.1, f32[8,8,512]{2,1,0:T(8,128)} %cot_in.1, f32[8,8,512]{2,1,0:T(8,128)} %dt_in.1, f32[8,8,512]{2,1,0:T(8,128)} %comp_in.1, f32[3,8,8,512]{3,2,1,0:T(8,128)} %trans_in.1, ...), custom_call_target="tpu_custom_call" | custom-call | tf_op jit(solution)/shard_map/pallas_call | solution.py:629
  27.9 0.0 copy-start
  27.9 1.6 %copy.13 = f32[8,8,512]{2,1,0:T(8,128)} copy(f32[8,8,512]{2,1,0:T(8,128)} %get-tuple-element.4) | data formatting | bytes 262144
  29.5 0.0 copy-done
  29.5 0.7 %copy.14 = f32[8,8,512]{2,1,0:T(8,128)} copy(f32[8,8,512]{2,1,0:T(8,128)S(1)} %copy-done) | data formatting | bytes 262144
Async XLA Ops:
  27.9 1.6 %copy-start = (f32[8,8,512]{2,1,0:T(8,128)S(1)}, f32[8,8,512]{2,1,0:T(8,128)}, u32[]{:S(2)}) copy-start(f32[8,8,512]{2,1,0:T(8,128)} %get-tuple-element.5) | copy-start | bytes 393220
